TPU v7x, 128 devices: a whole 4x4x4 slice. The times are simulated.
128 devices in a mesh: aux: 16 (over y, x), obat: 8 (over z, core).
Axes of the slice: x: 4, y: 4, z: 4, core: 2. Of those that a mesh axis runs over, the one named last changes fastest.
Arguments:
- half_factors: bfloat16 [2048, 128, 768], P('aux', 'obat'), may hold values from -2 to 2
- block_mask: int32 [128, 12], P('obat'), may hold values 0 or 1
- virt_coef: bfloat16 [768, 512], replicated, may hold values from -0.21875 to 0.21875
- occ_energy: float32 [128], replicated, may hold values from -2 to -0.4
- virt_energy: float32 [512], replicated, may hold values from 0.3 to 3
- pair_list: int32 [128, 6], replicated, may hold values from 0 to 127, as said below
- pair_count: int32 [128], replicated, may hold values from 1 to 6
Outputs:
- gamma_ao: float32 [2048, 128, 768], P('aux', 'obat')
Inputs may be any that keep to these rules, and one draw needn't show every extreme that they name: `pair_list`: row i holds 6 different orbitals j, each with j % 16 // 1 equal to i % 16; only its first pair_count[i] entries are used.
All inputs are finite; a program needn't handle non-finite values. No bound on the sum of `block_mask` on one device may be relied on, other than what follows from the above.
Results may differ from a plain program's by a relative error of at most 0.0037.
Values may be sent and summed in bfloat16 or wider, within the bound.
A program may use at most 128 MiB of HBM per device.

v0:
```python
import jax
import jax.numpy as jnp
from jax import lax
from jax.sharding import PartitionSpec as P

AOBLK = 64


def on_device(half_factors, block_mask, virt_coef, occ_energy, virt_energy, pair_list, pair_count):
    batch_rows = half_factors.shape[1]
    ao_width = half_factors.shape[2]
    blocks = block_mask.shape[1]
    expand = jnp.broadcast_to(block_mask[:, :, None], (batch_rows, blocks, AOBLK)).reshape(
        batch_rows, ao_width
    )
    masked = half_factors * expand.astype(jnp.bfloat16)[None, :, :]
    moved = lax.all_to_all(masked, "aux", split_axis=1, concat_axis=0, tiled=True)
    factors = jnp.einsum(
        "qim,ma->qia", moved, virt_coef, preferred_element_type=jnp.float32
    ).astype(jnp.bfloat16)
    group_rows = factors.shape[1]
    panels = lax.all_gather(factors, "obat", axis=1, tiled=True)
    first_orbital = lax.axis_index("obat") * batch_rows + lax.axis_index("aux") * group_rows
    orbital = first_orbital + 0
    own_panel = factors[:, 0, :]
    own_energy = lax.dynamic_index_in_dim(occ_energy, orbital, 0, keepdims=False)
    listed = lax.dynamic_index_in_dim(pair_list, orbital, 0, keepdims=False)
    counted = lax.dynamic_index_in_dim(pair_count, orbital, 0, keepdims=False)

    def add_pair(index, total, own_panel=own_panel, own_energy=own_energy, listed=listed):
        partner_id = lax.dynamic_index_in_dim(listed, index, 0, keepdims=False)
        position = partner_id // batch_rows * group_rows + partner_id % group_rows
        partner = lax.dynamic_index_in_dim(panels, position, 1, keepdims=False)
        integrals = lax.dot_general(
            own_panel, partner, (((0,), (0,)), ((), ())), preferred_element_type=jnp.float32
        )
        partner_energy = lax.dynamic_index_in_dim(occ_energy, partner_id, 0, keepdims=False)
        denom = own_energy + partner_energy - virt_energy[:, None] - virt_energy[None, :]
        amplitude = integrals / denom
        mixed = (2.0 * amplitude - amplitude.T).astype(jnp.bfloat16)
        return total + lax.dot_general(
            partner, mixed, (((1,), (1,)), ((), ())), preferred_element_type=jnp.float32
        )

    start = jnp.zeros((factors.shape[0], factors.shape[2]), jnp.float32)
    gamma_list = [lax.fori_loop(jnp.int32(0), counted, add_pair, start)]
    gamma_low = jnp.stack(gamma_list, axis=1).astype(jnp.bfloat16)
    gamma_wide = jnp.einsum("qia,ma->qim", gamma_low, virt_coef, preferred_element_type=jnp.float32)
    return lax.all_to_all(gamma_wide, "aux", split_axis=0, concat_axis=1, tiled=True)


def solution(mesh):
    in_specs = (P("aux", "obat", None), P("obat", None), P(), P(), P(), P(), P())
    out_specs = P("aux", "obat", None)
    return jax.shard_map(
        on_device, mesh=mesh, in_specs=in_specs, out_specs=out_specs, check_vma=False
    )
```

profile of v0, /device:TPU:0, one launch (start us, length us, event | category | flops | bytes accessed | tf_op | source)
XLA Modules:
  0.0 394.7 jit_solution(12640535961377310571)
XLA Ops:
  6.5 0.0 copy-start
  6.5 0.0 all-gather.3.cloned.1.call-start
  6.5 0.8 convert_element_type.27
  7.3 0.1 broadcast_in_dim.5
  7.4 0.1 convert_element_type.28
  7.5 3.7 copy_multiply_fusion
  11.2 46.5 %all_to_all.33 = bf16[128,16,768]{2,0,1:T(8,128)(2,1)S(1)} all-to-all(bf16[128,16,768]{2,0,1:T(8,128)(2,1)S(1)} %copy_multiply_fusion), channel_id=1, replica_groups=mesh['aux'=16,'obat'=8] {'aux'}, dimensions={1} | all-to-all | bytes 6291456 | tf_op jit(solution)/shard_map/all_to_all | solution.py:17
  57.8 0.0 copy-done
  57.8 0.0 copy-start.3
  57.8 0.0 copy-start.4
  57.8 0.0 copy-start.2
  57.8 3.2 convolution_convert_fusion
  61.0 0.0 all-gather.3.cloned.1.call-update
  61.0 0.0 copy-done.3
  61.0 0.7 dynamic_slice.33
  61.7 0.0 copy-done.4
  61.7 0.6 dynamic_slice.35
  62.2 0.0 copy-done.2
  62.2 0.2 dynamic-slice_reduce_fusion
  62.4 82.4 %all-gather.3.cloned.1.call-done = bf16[2048,4096]{1,0:T(8,128)(2,1)} async-done(((bf16[2048,512]{1,0:T(8,128)(2,1)}), bf16[2048,4096]{1,0:T(8,128)(2,1)}) %all-gather.3.cloned.1.call-update) | async-done | bytes 16777232 | tf_op jit(solution)/shard_map/all_gather | solution.py:22
  144.8 13.7 %copy.23 = bf16[256,8,8,512]{3,2,0,1:T(8,128)(2,1)} copy(bf16[256,8,8,512]{3,2,1,0:T(8,128)(2,1)} %bitcast.53) | data formatting | bytes 33554432 | tf_op jit(solution)/shard_map/all_gather | solution.py:22
  158.5 0.0 copy-start.1
  158.5 2.5 broadcast_in_dim.4
  161.1 0.0 copy-done.1
  161.1 34.1 %while.12 = (s32[]{:T(128)}, f32[2048,512]{1,0:T(8,128)}, s32[]{:T(128)}, s32[6]{0:T(128)S(1)}, bf16[2048,8,512]{2,0,1:T(8,128)(2,1)}, /*index=5*/bf16[2048,512]...) while((s32[]{:T(128)}, f32[2048,512]{1,0:T(8,128)}, ...), condition=%wide.region_1.2_spmd, body=%wide.region_0.1_spmd.sunk | while | flops 2150367744 | bytes 19935680 | solution.py:46
  161.8 0.6 dynamic_slice.51
  164.6 3.5 fusion.31
  168.1 0.3 copy.26
  169.6 0.6 dynamic_slice.52
  171.3 6.5 %convolution_add_fusion.2 = f32[2048,512]{1,0:T(8,128)} fusion(f32[2048,512]{1,0:T(8,128)} %get-tuple-element.234, bf16[2048,8,512]{2,0,1:T(8,128)(2,1)} %get-tuple-element.254, s32[]{:T(128)S(6)} %select_n.51, f32[512,512]{0,1:T(8,128)S(1)} %copy.26, f32[512,512]{1,0:T(8,128)S(1)} %fusion.31, f32[512]{0:T(512)S(1)} %get-tuple-element.258, ...), kind=kOutput, calls=%fused_computation.clone.1 | convolution fusion | flops 1076625408 | bytes 12591108 | tf_op jit(solution)/shard_map/while/body/dot_general | solution.py:41
  178.5 0.6 dynamic_slice.51
  181.3 3.5 fusion.31
  184.8 0.3 copy.26
  186.3 0.6 dynamic_slice.52
  188.0 6.5 %convolution_add_fusion.2 = f32[2048,512]{1,0:T(8,128)} fusion(f32[2048,512]{1,0:T(8,128)} %get-tuple-element.234, bf16[2048,8,512]{2,0,1:T(8,128)(2,1)} %get-tuple-element.254, s32[]{:T(128)S(6)} %select_n.51, f32[512,512]{0,1:T(8,128)S(1)} %copy.26, f32[512,512]{1,0:T(8,128)S(1)} %fusion.31, f32[512]{0:T(512)S(1)} %get-tuple-element.258, ...), kind=kOutput, calls=%fused_computation.clone.1 | convolution fusion | flops 1076625408 | bytes 12591108 | tf_op jit(solution)/shard_map/while/body/dot_general | solution.py:41
  195.2 4.0 %convolution_bitcast_fusion = f32[2048,1,768]{2,0,1:T(8,128)S(1)} fusion(bf16[768,512]{1,0:T(8,128)(2,1)S(1)} %copy-done, f32[2048,512]{1,0:T(8,128)} %get-tuple-element.123), kind=kOutput, calls=%fused_computation.21 | convolution fusion | flops 1611661312 | bytes 11272192 | tf_op jit(solution)/shard_map/qia,ma->qim/dot_general | solution.py:48
  199.2 35.1 %copy.17 = f32[2048,1,768]{2,1,0:T(1,128)S(1)} copy(f32[2048,1,768]{2,0,1:T(8,128)S(1)} %convolution_bitcast_fusion) | data formatting | bytes 12582912 | tf_op jit(solution)/shard_map/qia,ma->qim/dot_general | solution.py:48
  234.3 147.2 %all_to_all.34 = f32[2048,1,768]{2,1,0:T(1,128)S(1)} all-to-all(f32[2048,1,768]{2,1,0:T(1,128)S(1)} %copy.17), channel_id=1, replica_groups=mesh['aux'=16,'obat'=8] {'aux'}, dimensions={0} | all-to-all | bytes 12582912 | tf_op jit(solution)/shard_map/all_to_all | solution.py:49
  381.5 6.3 %copy.24 = f32[16,128,1,768]{3,0,1,2:T(8,128)} copy(f32[16,128,1,768]{3,2,1,0:T(1,128)S(1)} %bitcast.51) | data formatting | bytes 12582912 | tf_op jit(solution)/shard_map/all_to_all | solution.py:49
  (2 shorter events, 0.0 us)
Async XLA Ops:
  6.5 51.3 %copy-start = (bf16[768,512]{1,0:T(8,128)(2,1)S(1)}, bf16[768,512]{1,0:T(8,128)(2,1)}, u32[]{:S(2)}) copy-start(bf16[768,512]{1,0:T(8,128)(2,1)} %param.11) | copy-start | bytes 2359300
  6.5 138.2 %all-gather.3.cloned.1.call-start = ((), (), s32[]{:S(2)}) async-start(), calls=%async_computation.2 | async-start | bytes 18874368 | tf_op jit(solution)/shard_map/all_gather | solution.py:22
  57.8 3.2 copy-start.3
  57.8 3.9 copy-start.4
  57.8 4.4 %copy-start.2 = (s32[128,6]{0,1:T(8,128)S(1)}, s32[128,6]{0,1:T(8,128)}, u32[]{:S(2)}) copy-start(s32[128,6]{0,1:T(8,128)} %param.14) | copy-start | bytes 9220
  158.5 2.6 copy-start.1
Sparse Core Ops, SparseCore 0:
  61.1 83.6 all-gather.2
where the time goes:
time: 395 us
  blocking collectives  194 us (49%)
  waiting for transfers between devices  82.4 us (21%)
  local copies, waits for them, and re-layouts  62.3 us (16%)
  matrix products  27.1 us (7%)
  between operations  13.4 us (3%)
  loops' own time  11.2 us (3%)
  other arithmetic  4.5 us (1%)
    all_to_all x1, blocking collectives, on_device(): lax.all_to_all(gamma_wide, 'aux', split_axis=0, concat_axis=1, tiled=True)  147 us
    all_gather x1, waiting for transfers between devices, on_device(): panels = lax.all_gather(factors, 'obat', axis=1, tiled=True)  82.4 us
    all_to_all x1, blocking collectives, on_device(): lax.all_to_all(masked, 'aux', split_axis=1, concat_axis=0, tiled=True)  46.5 us
    dot_general x1, local copies, waits for them, and re-layouts, on_device(): jnp.einsum('qia,ma->qim', gamma_low, virt_coef, preferred_element_type=jn...  35.1 us
    all_gather x1, local copies, waits for them, and re-layouts, on_device(): panels = lax.all_gather(factors, 'obat', axis=1, tiled=True)  13.7 us
    dot_general x2, matrix products, add_pair(): lax.dot_general(partner, mixed, (((1,), (1,)), ((), ())), preferred_eleme...  12.9 us
    another operation x1, loops' own time, on_device(): gamma_list = [lax.fori_loop(jnp.int32(0), counted, add_pair, start)]  11.2 us
  transfers between devices with their start and end apart: 1, of which 1 were waited for; matrix products, arithmetic and copies ran while one was open for 0% of the time, Pallas kernels for 0%

commit v1 on v0

v1 whole, which is shorter than its diff:
```python
import jax
import jax.numpy as jnp
from jax import lax
from jax.sharding import PartitionSpec as P

AOBLK = 64


def on_device(half_factors, block_mask, virt_coef, occ_energy, virt_energy, pair_list, pair_count):
    batch_rows = half_factors.shape[1]
    expand = jnp.repeat(block_mask, AOBLK, axis=1).astype(jnp.bfloat16)
    masked = half_factors * expand[None, :, :]
    local = jnp.einsum(
        "pim,ma->ipa", masked, virt_coef, preferred_element_type=jnp.float32
    ).astype(jnp.bfloat16)
    own_panel = lax.all_to_all(local, "aux", split_axis=0, concat_axis=1, tiled=True)[0]
    panels = lax.all_gather(own_panel, "obat", axis=0, tiled=False)
    orbital = lax.axis_index("obat") * batch_rows + lax.axis_index("aux")
    own_energy = lax.dynamic_index_in_dim(occ_energy, orbital, 0, keepdims=False)
    listed = lax.dynamic_index_in_dim(pair_list, orbital, 0, keepdims=False)
    counted = lax.dynamic_index_in_dim(pair_count, orbital, 0, keepdims=False)

    def add_pair(index, total):
        partner_id = lax.dynamic_index_in_dim(listed, index, 0, keepdims=False)
        partner = lax.dynamic_index_in_dim(panels, partner_id // batch_rows, 0, keepdims=False)
        integrals = lax.dot_general(
            own_panel, partner, (((0,), (0,)), ((), ())), preferred_element_type=jnp.float32
        )
        partner_energy = lax.dynamic_index_in_dim(occ_energy, partner_id, 0, keepdims=False)
        denom = own_energy + partner_energy - virt_energy[:, None] - virt_energy[None, :]
        mixed = ((2.0 * integrals - integrals.T) / denom).astype(jnp.bfloat16)
        return total + lax.dot_general(
            partner, mixed, (((1,), (1,)), ((), ())), preferred_element_type=jnp.float32
        )

    start = jnp.zeros(own_panel.shape, jnp.float32)
    gamma = lax.fori_loop(jnp.int32(0), counted, add_pair, start)
    gamma_low = gamma.astype(jnp.bfloat16)[None]
    back = lax.all_to_all(gamma_low, "aux", split_axis=1, concat_axis=0, tiled=True)
    return jnp.einsum("ipa,ma->pim", back, virt_coef, preferred_element_type=jnp.float32)


def solution(mesh):
    in_specs = (P("aux", "obat", None), P("obat", None), P(), P(), P(), P(), P())
    out_specs = P("aux", "obat", None)
    return jax.shard_map(
        on_device, mesh=mesh, in_specs=in_specs, out_specs=out_specs, check_vma=False
    )
```

time: 395 us -> 331 us (0.84)
  the two profiles are of different devices: /device:TPU:0 before, /device:TPU:33 now
where the time goes in v1:
time: 331 us; the launch traced here: 330 us
  blocking collectives  151 us (46%)
  waiting for transfers between devices  83.3 us (25%)
  local copies, waits for them, and re-layouts  43.3 us (13%)
  other arithmetic  19.4 us (6%)
  matrix products  13.6 us (4%)
  between operations  13.5 us (4%)
  loops' own time  5.77 us (2%)
    all_to_all x1, blocking collectives, on_device(): lax.all_to_all(gamma_low, 'aux', split_axis=1, concat_axis=0, tiled=True)  117 us
    all_gather x1, waiting for transfers between devices, on_device(): panels = lax.all_gather(own_panel, 'obat', axis=0, tiled=False)  83.2 us
    all_to_all x1, blocking collectives, on_device(): lax.all_to_all(local, 'aux', split_axis=0, concat_axis=1, tiled=True)[0]  34.2 us
    broadcast_in_dim x1, local copies, waits for them, and re-layouts, on_device(): gamma_low = gamma.astype(jnp.bfloat16)[None]  18.5 us
    unnamed x1, other arithmetic  14 us
    unnamed x14, local copies, waits for them, and re-layouts  12.8 us
  transfers between devices with their start and end apart: 1, of which 1 were waited for; matrix products, arithmetic and copies ran while one was open for 0% of the time, Pallas kernels for 0%

profile of v1, /device:TPU:33, one launch (start us, length us, event | category | flops | bytes accessed | tf_op | source)
XLA Modules:
  0.0 329.7 jit_solution(12743000259237545582)
XLA Ops:
  6.5 0.0 copy-start
  6.5 0.0 all-gather.2.cloned.1.call-start
  6.5 0.8 convert_element_type.26
  7.3 0.1 broadcast_in_dim.13
  7.4 0.1 convert_element_type.27
  7.5 2.1 broadcast_multiply_fusion
  9.6 0.0 copy-done
  9.6 2.0 convert_bitcast_fusion.1
  11.6 0.0 copy-start.3
  11.6 0.0 copy-start.4
  11.7 0.0 copy-start.2
  11.7 34.2 %all_to_all.24 = bf16[16,128,512]{2,1,0:T(8,128)(2,1)} all-to-all(bf16[16,128,512]{2,1,0:T(8,128)(2,1)S(1)} %convert_bitcast_fusion.1), channel_id=1, replica_groups=mesh['aux'=16,'obat'=8] {'aux'}, dimensions={0} | all-to-all | bytes 4194304 | tf_op jit(solution)/shard_map/all_to_all | solution.py:16
  45.8 0.0 copy-start.1
  45.8 0.0 all-gather.2.cloned.1.call-update
  45.9 0.0 copy-done.3
  45.9 0.6 dynamic_slice.33
  46.5 0.0 copy-done.4
  46.5 0.6 dynamic_slice.35
  47.1 0.0 copy-done.2
  47.1 0.2 dynamic-slice_reduce_fusion
  47.3 83.2 %all-gather.2.cloned.1.call-done = bf16[8,2048,512]{2,1,0:T(8,128)(2,1)} async-done(((bf16[1,2048,512]{2,1,0:T(8,128)(2,1)}), bf16[8,2048,512]{2,1,0:T(8,128)(2,1)}) %all-gather.2.cloned.1.call-update) | async-done | bytes 16777232 | tf_op jit(solution)/shard_map/all_gather | solution.py:17
  130.5 2.5 broadcast_in_dim.12
  133.1 0.0 copy-done.1
  133.1 17.0 %while.12 = (s32[]{:T(128)}, f32[2048,512]{1,0:T(8,128)}, s32[]{:T(128)}, s32[6]{0:T(128)S(1)}, bf16[8,2048,512]{2,1,0:T(8,128)(2,1)}, /*index=5*/bf16[2048,512]...) while((s32[]{:T(128)}, f32[2048,512]{1,0:T(8,128)}, ...), condition=%wide.region_1.2_spmd, body=%wide.region_0.1_spmd.sunk | while | flops 2149843456 | bytes 19931584 | solution.py:37
  133.7 0.6 dynamic_slice.51
  136.5 3.5 %fusion.31 = f32[512,512]{1,0:T(8,128)S(1)} fusion(bf16[2048,512]{1,0:T(8,128)(2,1)} %get-tuple-element.236, bf16[8,2048,512]{2,1,0:T(8,128)(2,1)} %get-tuple-element.235, s32[]{:T(128)S(6)} %select_n.44), kind=kOutput, calls=%fused_computation.2.clone.1 | convolution fusion | flops 1073741824 | bytes 5242884 | tf_op jit(solution)/shard_map/while/body/dot_general | solution.py:26
  140.0 0.3 copy.29
  141.4 0.6 dynamic_slice.52
  143.2 6.3 %convolution_add_fusion.2 = f32[2048,512]{1,0:T(8,128)} fusion(f32[2048,512]{1,0:T(8,128)} %get-tuple-element.215, bf16[8,2048,512]{2,1,0:T(8,128)(2,1)} %get-tuple-element.235, s32[]{:T(128)S(6)} %select_n.44, f32[512,512]{1,0:T(8,128)S(1)} %fusion.31, f32[512,512]{0,1:T(8,128)S(1)} %copy.29, f32[512]{0:T(512)S(1)} %get-tuple-element.239, ...), kind=kOutput, calls=%fused_computation.clone.1 | convolution fusion | flops 1076101120 | bytes 12587012 | tf_op jit(solution)/shard_map/while/body/dot_general | solution.py:32
  150.1 2.5 convert_bitcast_fusion
  152.6 18.5 %copy.27 = bf16[1,2048,512]{2,0,1:T(2,128)(2,1)} copy(bf16[1,2048,512]{2,1,0:T(8,128)(2,1)S(1)} %convert_bitcast_fusion) | data formatting | bytes 4194304 | tf_op jit(solution)/shard_map/broadcast_in_dim | solution.py:38
  171.1 0.5 broadcast.24
  171.6 14.0 %reduce.2 = bf16[2048,512]{1,0:T(8,128)(2,1)S(1)} reduce(bf16[2048,1,512]{2,1,0:T(2,128)(2,1)} %bitcast.48, bf16[]{:T(256)} %broadcast.24), dimensions={1}, to_apply=%bitcast.35.reduce_sub_computation | reduce | bytes 4194306
  185.7 2.8 reshape.22
  188.4 116.8 %all_to_all.25 = bf16[16,2,32768]{2,1,0:T(2,128)(2,1)S(1)} all-to-all(bf16[16,2,32768]{2,1,0:T(2,128)(2,1)} %reshape.22), channel_id=1, replica_groups=mesh['aux'=16,'obat'=8] {'aux'}, dimensions={0} | all-to-all | bytes 4194304 | tf_op jit(solution)/shard_map/all_to_all | solution.py:39
  305.2 6.7 %reshape.23 = bf16[2048,1,512]{2,1,0:T(2,128)(2,1)} reshape(bf16[16,2,32768]{2,1,0:T(2,128)(2,1)S(1)} %all_to_all.25) | data formatting | bytes 4194304
  311.9 2.8 copy.21
  314.7 1.8 convolution_bitcast_fusion
  316.6 6.3 %copy.20 = f32[128,16,768]{2,1,0:T(8,128)} copy(f32[128,16,768]{2,0,1:T(8,128)S(1)} %convolution_bitcast_fusion) | data formatting | bytes 12582912 | tf_op jit(solution)/shard_map/ipa,ma->pim/transpose | solution.py:40
  (1 shorter events, 0.0 us)
Async XLA Ops:
  6.5 3.1 copy-start
  6.5 124.0 %all-gather.2.cloned.1.call-start = ((), (), s32[]{:S(2)}) async-start(), calls=%async_computation.2 | async-start | bytes 18874368 | tf_op jit(solution)/shard_map/all_gather | solution.py:17
  11.6 34.2 %copy-start.3 = (s32[128]{0:T(128)S(1)}, s32[128]{0:T(128)}, u32[]{:S(2)}) copy-start(s32[128]{0:T(128)} %param.15) | copy-start | bytes 1540
  11.6 34.8 %copy-start.4 = (f32[128]{0:T(128)S(1)}, f32[128]{0:T(128)}, u32[]{:S(2)}) copy-start(f32[128]{0:T(128)} %param.12) | copy-start | bytes 1540
  11.7 35.4 %copy-start.2 = (s32[128,6]{0,1:T(8,128)S(1)}, s32[128,6]{0,1:T(8,128)}, u32[]{:S(2)}) copy-start(s32[128,6]{0,1:T(8,128)} %param.14) | copy-start | bytes 9220
  45.8 87.2 %copy-start.1 = (f32[512]{0:T(512)S(1)}, f32[512]{0:T(512)}, u32[]{:S(2)}) copy-start(f32[512]{0:T(512)} %param.13) | copy-start | bytes 6148
Sparse Core Ops, SparseCore 0:
  46.0 84.4 all-gather.1

commit v2 on v1

v2 whole, which is shorter than its diff:
```python
import functools

import jax
import jax.numpy as jnp
from jax import lax
from jax.experimental import pallas as pl
from jax.experimental.pallas import tpu as pltpu
from jax.sharding import PartitionSpec as P

AOBLK = 64
SIDE = 4
LAG = (1, 3, 5, 6)
MESH = pl.DeviceIdType.MESH


def dot(a, b):
    return lax.dot_general(a, b, (((1,), (0,)), ((), ())), preferred_element_type=jnp.float32)


def pair_kernel(
    sums, weight, virt_row, virt_col, local, out,
    panels, total, recip, mixed, gamma,
    a_send, a_recv, u_send, u_recv, d_send, d_recv, f_send, f_recv, s_send, s_recv, r_send, r_recv,
):
    aux = lax.axis_index("aux")
    obat = lax.axis_index("obat")
    y, x = aux // SIDE, aux % SIDE
    z, core = obat // 2, obat % 2
    rounds, slab = local.shape[0], local.shape[1]
    nvir = local.shape[2]
    slots = panels.shape[0]
    above = (aux, (z + 1) % SIDE * 2 + core)
    below = (aux, (z + SIDE - 1) % SIDE * 2 + core)
    sibling = (aux, z * 2 + 1 - core)
    chunks = rounds // 2
    wide = 2 * slab

    def target(r):
        return (y + r // SIDE) % SIDE * SIDE + (x + r % SIDE) % SIDE

    def source(r):
        return (y + SIDE - r // SIDE) % SIDE * SIDE + (x + SIDE - r % SIDE) % SIDE

    def rows(r):
        return pl.ds(pl.multiple_of(r * slab, slab), slab)

    def push(src, dst, send, recv, device):
        return pltpu.make_async_remote_copy(
            src_ref=src, dst_ref=dst, send_sem=send, recv_sem=recv,
            device_id=device, device_id_type=MESH,
        )

    def scatter(r):
        return push(local.at[target(r)], panels.at[0, rows(r)], a_send.at[r], a_recv.at[r], (target(r), obat))

    def upward(r):
        return push(panels.at[0, rows(r)], panels.at[2, rows(r)], u_send.at[r], u_recv.at[r], above)

    def downward(r):
        return push(panels.at[0, rows(r)], panels.at[4, rows(r)], d_send.at[r], d_recv.at[r], below)

    def further_up(r):
        return push(panels.at[2, rows(r)], panels.at[6, rows(r)], f_send.at[r], f_recv.at[r], above)

    def further_down(r):
        return push(panels.at[4, rows(r)], panels.at[6, rows(r)], f_send.at[r], f_recv.at[r], below)

    def across(k, r):
        return push(
            panels.at[2 * k, rows(r)], panels.at[2 * k + 1, rows(r)],
            s_send.at[k, r], s_recv.at[k, r], sibling,
        )

    def back(r):
        return push(gamma.at[rows(r)], out.at[aux], r_send.at[r], r_recv.at[r], (source(r), obat))

    barrier = pltpu.get_barrier_semaphore()

    def greet(r, carry):
        pl.semaphore_signal(barrier, inc=1, device_id=(target(r), obat), device_id_type=MESH)
        return carry

    lax.fori_loop(1, rounds, greet, 0)
    for device in (above, below, sibling):
        pl.semaphore_signal(barrier, inc=1, device_id=device, device_id_type=MESH)
    pl.semaphore_wait(barrier, rounds + 2)

    def send_out(r, carry):
        scatter(r).start()
        return carry

    lax.fori_loop(1, rounds, send_out, 0)
    panels[0, pl.ds(0, slab), :] = local[aux]

    def prepare(s, carry):
        total[s] = jnp.zeros((nvir, nvir), jnp.float32)
        denom = (sums[s] - virt_col[...]) - virt_row[...]
        recip[s] = weight[s] / denom
        return carry

    def pair_up(k, c):
        part = pl.ds(pl.multiple_of(c * wide, wide), wide)
        own = panels[0, part, :]
        flipped = (-own).T
        for s in (2 * k, 2 * k + 1):
            other = panels[s, part, :]
            total[s] += dot((2 * other).T, own) + dot(flipped, other)

    def stage(c, carry):
        @pl.when(c < chunks)
        def _():
            for h in range(2):
                r = 2 * c + h
                if h == 0:
                    @pl.when(r > 0)
                    def _():
                        scatter(r).wait_recv()
                else:
                    scatter(r).wait_recv()
                upward(r).start()
                downward(r).start()
                across(0, r).start()

        @pl.when((c >= LAG[0]) & (c < chunks + LAG[0]))
        def _():
            for h in range(2):
                r = 2 * (c - LAG[0]) + h
                upward(r).wait_recv()
                downward(r).wait_recv()
                if h == 0:
                    further_up(r).start()
                else:
                    further_down(r).start()
                across(1, r).start()
                across(2, r).start()

        @pl.when(c == 0)
        def _():
            lax.fori_loop(0, slots, prepare, 0)

        @pl.when((c >= LAG[0]) & (c < chunks + LAG[0]))
        def _():
            b = c - LAG[0]
            for h in range(2):
                across(0, 2 * b + h).wait_recv()
            pair_up(0, b)

        @pl.when((c >= LAG[1]) & (c < chunks + LAG[1]))
        def _():
            b = c - LAG[1]
            for h in range(2):
                further_up(2 * b + h).wait_recv()
                across(3, 2 * b + h).start()
            for k in (1, 2):
                for h in range(2):
                    across(k, 2 * b + h).wait_recv()
                pair_up(k, b)

        @pl.when((c >= LAG[2]) & (c < chunks + LAG[2]))
        def _():
            b = c - LAG[2]
            for h in range(2):
                across(3, 2 * b + h).wait_recv()
            pair_up(3, b)

        return carry

    lax.fori_loop(0, chunks + LAG[2], stage, 0)

    def finish(s, carry):
        mixed[s] = (total[s] * recip[s]).astype(jnp.bfloat16)
        return carry

    lax.fori_loop(0, slots, finish, 0)

    def collect(q, carry):
        quarter = rounds // SIDE - 1 - q
        part = pl.ds(pl.multiple_of(quarter * SIDE * slab, SIDE * slab), SIDE * slab)
        for n in range(2):
            cols = pl.ds(n * (nvir // 2), nvir // 2)
            acc = dot(panels[0, part, :], mixed[0, :, cols])
            for s in range(1, slots):
                acc += dot(panels[s, part, :], mixed[s, :, cols])
            gamma[part, cols] = acc.astype(jnp.bfloat16)
        for h in range(SIDE):
            r = quarter * SIDE + h
            if h == 0:
                @pl.when(r > 0)
                def _():
                    back(r).start()
            else:
                back(r).start()
        return carry

    lax.fori_loop(0, rounds // SIDE, collect, 0)
    own_copy = pltpu.make_async_copy(gamma.at[pl.ds(0, slab)], out.at[aux], r_send.at[0])
    own_copy.start()

    def settle(r, carry):
        upward(r).wait_send()
        downward(r).wait_send()
        further_up(r).wait_send()
        for k in range(slots // 2):
            across(k, r).wait_send()
        return carry

    lax.fori_loop(0, rounds, settle, 0)

    def close(r, carry):
        scatter(r).wait_send()
        back(r).wait()
        return carry

    own_copy.wait()
    lax.fori_loop(1, rounds, close, 0)


def on_device(half_factors, block_mask, virt_coef, occ_energy, virt_energy, pair_list, pair_count):
    slab, batch_rows, _ = half_factors.shape
    nvir = virt_coef.shape[1]
    expand = jnp.repeat(block_mask, AOBLK, axis=1).astype(jnp.bfloat16)
    masked = half_factors * expand[None, :, :]
    local = jnp.einsum(
        "pim,ma->ipa", masked, virt_coef, preferred_element_type=jnp.float32
    ).astype(jnp.bfloat16)

    aux, obat = lax.axis_index("aux"), lax.axis_index("obat")
    z, core = obat // 2, obat % 2
    orbital = obat * batch_rows + aux
    step = jnp.array([0, 0, -1, -1, 1, 1, 2, 2], jnp.int32)
    other = jnp.array([0, 1] * 4, jnp.int32)
    batch = (z + step + SIDE) % SIDE * 2 + (core + other) % 2
    member = batch * batch_rows + aux
    sums = occ_energy[orbital] + occ_energy[member]
    used = jnp.arange(pair_list.shape[1]) < pair_count[orbital]
    weight = jnp.any((pair_list[orbital][None, :] == member[:, None]) & used[None, :], axis=1)
    weight = weight.astype(jnp.float32)

    rounds, slots = batch_rows, 8
    length = rounds * slab
    dma = pltpu.SemaphoreType.DMA
    smem = pl.BlockSpec(memory_space=pltpu.SMEM)
    vmem = pl.BlockSpec(memory_space=pltpu.VMEM)
    back = pl.pallas_call(
        pair_kernel,
        out_shape=jax.ShapeDtypeStruct((rounds, slab, nvir), jnp.bfloat16),
        in_specs=[smem, smem, vmem, vmem, vmem],
        out_specs=pl.BlockSpec(memory_space=pl.ANY),
        scratch_shapes=[
            pltpu.VMEM((slots, length, nvir), jnp.bfloat16),
            pltpu.VMEM((slots, nvir, nvir), jnp.float32),
            pltpu.VMEM((slots, nvir, nvir), jnp.float32),
            pltpu.VMEM((slots, nvir, nvir), jnp.bfloat16),
            pltpu.VMEM((length, nvir), jnp.bfloat16),
        ]
        + [dma((rounds,))] * 8
        + [dma((slots // 2, rounds))] * 2
        + [dma((rounds,))] * 2,
        compiler_params=pltpu.CompilerParams(
            collective_id=0, has_side_effects=True, vmem_limit_bytes=60 * 1024 * 1024
        ),
    )(sums, weight, virt_energy[None, :], virt_energy[:, None], local)
    return jnp.einsum("ipa,ma->pim", back, virt_coef, preferred_element_type=jnp.float32)


def solution(mesh):
    in_specs = (P("aux", "obat", None), P("obat", None), P(), P(), P(), P(), P())
    out_specs = P("aux", "obat", None)
    return jax.shard_map(
        on_device, mesh=mesh, in_specs=in_specs, out_specs=out_specs, check_vma=False
    )
```

time: 331 us -> 147 us (0.44)
  the two profiles are of different devices: /device:TPU:33 before, /device:TPU:0 now
where the time goes in v2:
time: 147 us; the launch traced here: 146 us
  Pallas kernels  120 us (82%)
  local copies, waits for them, and re-layouts  12.9 us (9%)
  matrix products  6.74 us (5%)
  other arithmetic  6.06 us (4%)
    pallas_call x1, Pallas kernels, on_device(): pl.pallas_call(pair_kernel, out_shape=jax.ShapeDtypeStruct((rounds, slab,...  120 us
    transpose x1, local copies, waits for them, and re-layouts, on_device(): jnp.einsum('ipa,ma->pim', back, virt_coef, preferred_element_type=jnp.flo...  6.35 us
    dot_general x1, matrix products, on_device(): jnp.einsum('ipa,ma->pim', back, virt_coef, preferred_element_type=jnp.flo...  3.42 us
    dot_general x1, matrix products, on_device(): jnp.einsum('pim,ma->ipa', masked, virt_coef, preferred_element_type=jnp.f...  3.31 us

profile of v2, /device:TPU:0, one launch (start us, length us, event | category | flops | bytes accessed | tf_op | source)
XLA Modules:
  0.0 146.0 jit_solution(540780027583638814)
XLA Ops:
  0.0 0.0 copy-start
  0.0 1.3 dynamic_slice.9
  1.3 1.3 dynamic_slice.11
  2.6 0.7 iota_compare_fusion
  3.3 0.9 dynamic-slice_reduce_fusion
  4.2 0.7 compare_select_fusion
  4.9 0.2 and_reduce_fusion
  5.1 0.5 convert_element_type.19.weight
  5.6 1.3 gather_fusion
  6.9 1.2 broadcast_add_fusion.sums
  8.1 0.7 convert_element_type.20
  8.8 0.1 broadcast_in_dim.18
  8.9 0.1 convert_element_type.21
  9.0 1.6 %copy.14.virt_col = f32[512,1]{1,0:T(8,128)} copy(f32[512,1]{0,1:T(1,128)} %bitcast.14) | data formatting | bytes 4096 | tf_op jit(solution)/shard_map/broadcast_in_dim | solution.py:262
  10.5 2.1 %broadcast_multiply_fusion = bf16[128,16,768]{2,1,0:T(8,128)(2,1)S(1)} fusion(bf16[128,16,768]{2,1,0:T(8,128)(2,1)} %param.9, bf16[16,768]{1,0:T(8,128)(2,1)S(1)} %convert_element_type.21), kind=kLoop, calls=%fused_computation.5 | loop fusion | flops 1572864 | bytes 6316032 | tf_op jit(solution)/shard_map/mul | solution.py:222
  12.6 0.0 copy-done
  12.7 3.3 %convert_bitcast_fusion.local = bf16[16,128,512]{2,1,0:T(8,128)(2,1)} fusion(bf16[128,16,768]{2,1,0:T(8,128)(2,1)S(1)} %broadcast_multiply_fusion, bf16[768,512]{1,0:T(8,128)(2,1)S(1)} %copy-done), kind=kOutput, calls=%fused_computation.4 | convolution fusion | flops 1611661312 | bytes 6029312 | tf_op jit(solution)/shard_map/pim,ma->ipa/dot_general | solution.py:223
  16.0 120.3 %shard_map.91 = bf16[16,128,512]{2,1,0:T(8,128)(2,1)} custom-call(f32[8]{0:T(128)} %broadcast_add_fusion.sums, f32[8]{0:T(128)} %convert_element_type.19.weight, f32[1,512]{1,0:T(1,128)} %bitcast.15, f32[512,1]{1,0:T(8,128)} %copy.14.virt_col, bf16[16,128,512]{2,1,0:T(8,128)(2,1)} %convert_bitcast_fusion.local), custom_call_target="tpu_custom_call" | custom-call | tf_op jit(solution)/shard_map/pallas_call | solution.py:244
  136.2 3.4 %convolution_bitcast_fusion = f32[128,16,768]{2,0,1:T(8,128)S(1)} fusion(bf16[16,128,512]{2,1,0:T(8,128)(2,1)} %shard_map.91, bf16[768,512]{1,0:T(8,128)(2,1)S(1)} %copy-done), kind=kOutput, calls=%fused_computation.3 | convolution fusion | flops 1610612736 | bytes 9175040 | tf_op jit(solution)/shard_map/ipa,ma->pim/dot_general | solution.py:263
  139.7 6.3 %copy.15 = f32[128,16,768]{2,1,0:T(8,128)} copy(f32[128,16,768]{2,0,1:T(8,128)S(1)} %convolution_bitcast_fusion) | data formatting | bytes 12582912 | tf_op jit(solution)/shard_map/ipa,ma->pim/transpose | solution.py:263
  (1 shorter events, 0.0 us)
Async XLA Ops:
  0.0 12.6 %copy-start = (bf16[768,512]{1,0:T(8,128)(2,1)S(1)}, bf16[768,512]{1,0:T(8,128)(2,1)}, u32[]{:S(2)}) copy-start(bf16[768,512]{1,0:T(8,128)(2,1)} %param.11) | copy-start | bytes 2359300

commit v3 on v2

v3 whole, which is shorter than its diff:
```python
import jax
import jax.numpy as jnp
from jax import lax
from jax.experimental import pallas as pl
from jax.experimental.pallas import tpu as pltpu
from jax.sharding import PartitionSpec as P

AOBLK = 64
SIDE = 4
AHEAD = 3
LAG_NEAR, LAG_FAR = 1, 2
LOADS = 4
MESH = pl.DeviceIdType.MESH


def dot(a, b, contract=((1,), (0,))):
    return lax.dot_general(a, b, (contract, ((), ())), preferred_element_type=jnp.float32)


def pair_kernel(
    occ, listed, counted, mask, virt_row, virt, half, out,
    half_vm, wide_f, local, panels, total, recip, mixed, share, opposite, gamma, virt_col, sums, weight,
    l_sem, a_send, a_recv, m_send, m_recv, p_send, p_recv, s_send, s_recv, g_send, g_recv, r_send, r_recv,
):
    aux = lax.axis_index("aux")
    obat = lax.axis_index("obat")
    y, x = aux // SIDE, aux % SIDE
    z, core = obat // 2, obat % 2
    rounds, slab, nvir = local.shape
    slots = total.shape[0]
    lanes = nvir // 128
    chunks = rounds // 2
    wide = 2 * slab
    z_one = (z + SIDE - 1 + 2 * core) % SIDE
    z_two = (z + 1 + 2 * core) % SIDE
    one = (aux, z_one * 2 + core)
    two = (aux, z_two * 2 + core)
    sibling = (aux, z * 2 + 1 - core)

    def shift(r):
        return (r + r // SIDE) % SIDE, r % SIDE

    def target(r):
        dy, dx = shift(r)
        return (y + dy) % SIDE * SIDE + (x + dx) % SIDE

    def source(r):
        dy, dx = shift(r)
        return (y + SIDE - dy) % SIDE * SIDE + (x + SIDE - dx) % SIDE

    def rows(r):
        return pl.ds(pl.multiple_of(r * slab, slab), slab)

    def push(src, dst, send, recv, device):
        return pltpu.make_async_remote_copy(
            src_ref=src, dst_ref=dst, send_sem=send, recv_sem=recv,
            device_id=device, device_id_type=MESH,
        )

    def scatter(r):
        return push(local.at[r], panels.at[0, rows(r)], a_send.at[r], a_recv.at[r], (target(r), obat))

    def to_one(r):
        return push(panels.at[0, rows(r)], panels.at[4, rows(r)], m_send.at[r], m_recv.at[r], one)

    def to_two(r):
        return push(panels.at[0, rows(r)], panels.at[2, rows(r)], p_send.at[r], p_recv.at[r], two)

    def across(k, r):
        return push(
            panels.at[2 * k, rows(r)], panels.at[(1, 5, 3)[k], rows(r)],
            s_send.at[k, r], s_recv.at[k, r], sibling,
        )

    def give(r):
        return push(share.at[rows(r)], opposite.at[rows(r)], g_send.at[r], g_recv.at[r], one)

    def back(r):
        return push(gamma.at[rows(r)], out.at[aux], r_send.at[r], r_recv.at[r], (source(r), obat))

    piece = slab // LOADS

    def load(n):
        part = pl.ds(n * piece, piece)
        return pltpu.make_async_copy(half.at[part], half_vm.at[part], l_sem.at[n])

    for n in range(LOADS):
        load(n).start()

    barrier = pltpu.get_barrier_semaphore()

    def greet(r, carry):
        pl.semaphore_signal(barrier, inc=1, device_id=(target(r), obat), device_id_type=MESH)
        return carry

    lax.fori_loop(1, rounds, greet, 0)
    for device in (one, two, sibling):
        pl.semaphore_signal(barrier, inc=1, device_id=device, device_id_type=MESH)

    blocks = mask.shape[1]
    nao = virt.shape[0]
    spread = lax.broadcasted_iota(jnp.int32, (blocks, nao), 1) // AOBLK
    spread = (spread == lax.broadcasted_iota(jnp.int32, (blocks, nao), 0)).astype(jnp.bfloat16)
    keep = dot(mask[...].astype(jnp.bfloat16), spread).astype(jnp.bfloat16)
    for n in range(LOADS):
        load(n).wait()
        block = half_vm[pl.ds(n * piece, piece)] * keep[None]
        block = block.reshape(piece * rounds, nao)
        product = dot(block, virt[...])
        for w in range(lanes):
            wide_f[w, pl.ds(n * piece * rounds, piece * rounds), :] = product[:, w * 128 : (w + 1) * 128]

    def pick(r):
        parts = [wide_f[w, pl.ds(target(r), slab, stride=rounds), :] for w in range(lanes)]
        return jnp.concatenate(parts, axis=1).astype(jnp.bfloat16)

    panels[0, pl.ds(0, slab), :] = pick(0)
    pl.semaphore_wait(barrier, rounds + 2)

    def send_out(r, carry):
        local[r] = pick(r)
        scatter(r).start()
        return carry

    lax.fori_loop(1, 2 * AHEAD, send_out, 0)

    def orbital(level, side):
        return (level * 2 + side) * rounds + aux

    mine, foreign = orbital(z, core), orbital(z_one, core)
    couples = [(mine, orbital(level, side)) for level in (z, z_one, z_two) for side in (core, 1 - core)]
    couples += [(foreign, orbital(z_two, side)) for side in (core, 1 - core)]

    def prepare_scalars():
        for s, (i, j) in enumerate(couples):
            sums[s] = occ[i] + occ[j]
            hit = jnp.int32(0)
            for p in range(listed.shape[1]):
                hit += jnp.where((listed[i, p] == j) & (p < counted[i]), 1, 0)
            weight[s] = hit.astype(jnp.float32)

    def prepare(s, carry):
        total[s] = jnp.zeros((nvir, nvir), jnp.float32)
        for n in range(nvir // 128):
            cols = pl.ds(n * 128, 128)
            denom = (sums[s] - virt_col[...]) - virt_row[:, cols]
            recip[s, :, cols] = weight[s] / denom
        return carry

    def pair_up(c, held, fixed, others):
        part = pl.ds(pl.multiple_of(c * wide, wide), wide)
        own = panels[fixed, part, :]
        flipped = (-own).T
        for t, s in zip(held, others):
            other = panels[s, part, :]
            total[t] += dot((2 * other).T, own) + dot(flipped, other)

    def stage(c, carry):
        @pl.when(c < chunks)
        def _():
            for h in range(2):
                r = 2 * c + h
                if h == 0:
                    @pl.when(r > 0)
                    def _():
                        scatter(r).wait_recv()
                else:
                    scatter(r).wait_recv()
                to_one(r).start()
                to_two(r).start()
                across(0, r).start()

        @pl.when(c + AHEAD < chunks)
        def _():
            for h in range(2):
                send_out(2 * (c + AHEAD) + h, 0)

        @pl.when((c >= LAG_NEAR) & (c < chunks + LAG_NEAR))
        def _():
            for h in range(2):
                r = 2 * (c - LAG_NEAR) + h
                to_two(r).wait_recv()
                across(1, r).start()
                to_one(r).wait_recv()
                across(2, r).start()

        @pl.when(c == 0)
        def _():
            virt_col[...] = jnp.broadcast_to(virt_row[...], (128, nvir)).T
            prepare_scalars()
            lax.fori_loop(0, slots, prepare, 0)

        @pl.when((c >= LAG_NEAR) & (c < chunks + LAG_NEAR))
        def _():
            b = c - LAG_NEAR
            for h in range(2):
                across(0, 2 * b + h).wait_recv()
            pair_up(b, (0, 1, 2, 4), 0, (0, 1, 2, 4))
            pair_up(b, (6,), 2, (4,))

        @pl.when(c >= LAG_FAR)
        def _():
            b = c - LAG_FAR
            for h in range(2):
                across(1, 2 * b + h).wait_recv()
                across(2, 2 * b + h).wait_recv()
            pair_up(b, (3, 5), 0, (3, 5))
            pair_up(b, (7,), 2, (5,))

        return carry

    lax.fori_loop(0, chunks + LAG_FAR, stage, 0)

    def finish(t, carry):
        s = slots - 1 - t
        mixed[s] = (total[s] * recip[s]).astype(jnp.bfloat16)
        return carry

    lax.fori_loop(0, slots, finish, 0)

    halves = [pl.ds(n * (nvir // 2), nvir // 2) for n in range(2)]

    def hand_over(q, carry):
        length = SIDE * slab
        quarter = rounds // SIDE - 1 - q
        part = pl.ds(pl.multiple_of(quarter * length, length), length)
        for cols in halves:
            acc = dot(panels[4, part, :], mixed[6, :, cols]) + dot(panels[5, part, :], mixed[7, :, cols])
            share[part, cols] = acc.astype(jnp.bfloat16)
        for h in range(SIDE):
            give(quarter * SIDE + SIDE - 1 - h).start()
        return carry

    lax.fori_loop(0, rounds // SIDE, hand_over, 0)

    def collect(q, carry):
        c = chunks - 1 - q
        part = pl.ds(pl.multiple_of(c * wide, wide), wide)
        give(2 * c + 1).wait_recv()
        give(2 * c).wait_recv()
        for cols in halves:
            acc = opposite[part, cols].astype(jnp.float32)
            for s in range(6):
                acc += dot(panels[s, part, :], mixed[s, :, cols])
            gamma[part, cols] = acc.astype(jnp.bfloat16)
        back(2 * c + 1).start()

        @pl.when(c > 0)
        def _():
            back(2 * c).start()

        return carry

    lax.fori_loop(0, chunks, collect, 0)
    own_copy = pltpu.make_async_copy(gamma.at[pl.ds(0, slab)], out.at[aux], r_send.at[0])
    own_copy.start()

    def settle(r, carry):
        to_one(r).wait_send()
        to_two(r).wait_send()
        give(r).wait_send()
        for k in range(3):
            across(k, r).wait_send()
        return carry

    lax.fori_loop(0, rounds, settle, 0)

    def close(r, carry):
        scatter(r).wait_send()
        back(r).wait()
        return carry

    own_copy.wait()
    lax.fori_loop(1, rounds, close, 0)


def last_kernel(back, virt, out, mixed_rows):
    batch_rows, part, nvir = back.shape
    nao = virt.shape[0]
    product = dot(back[...].reshape(batch_rows * part, nvir), virt[...], ((1,), (1,)))
    for w in range(nao // 128):
        cols = slice(w * 128, (w + 1) * 128)
        for i in range(batch_rows):
            mixed_rows[w, pl.ds(i, part, stride=batch_rows), :] = product[i * part : (i + 1) * part, cols]
        out[:, cols] = mixed_rows[w]


def on_device(half_factors, block_mask, virt_coef, occ_energy, virt_energy, pair_list, pair_count):
    slab, rounds, nao = half_factors.shape
    nvir = virt_coef.shape[1]
    slots = 8
    length = rounds * slab
    dma = pltpu.SemaphoreType.DMA
    smem = pl.BlockSpec(memory_space=pltpu.SMEM)
    vmem = pl.BlockSpec(memory_space=pltpu.VMEM)
    anywhere = pl.BlockSpec(memory_space=pl.ANY)
    back = pl.pallas_call(
        pair_kernel,
        out_shape=jax.ShapeDtypeStruct((rounds, slab, nvir), jnp.bfloat16),
        in_specs=[smem, smem, smem, vmem, vmem, vmem, anywhere],
        out_specs=anywhere,
        scratch_shapes=[
            pltpu.VMEM((slab, rounds, nao), jnp.bfloat16),
            pltpu.VMEM((nvir // 128, length, 128), jnp.float32),
            pltpu.VMEM((rounds, slab, nvir), jnp.bfloat16),
            pltpu.VMEM((6, length, nvir), jnp.bfloat16),
            pltpu.VMEM((slots, nvir, nvir), jnp.float32),
            pltpu.VMEM((slots, nvir, nvir), jnp.float32),
            pltpu.VMEM((slots, nvir, nvir), jnp.bfloat16),
            pltpu.VMEM((length, nvir), jnp.bfloat16),
            pltpu.VMEM((length, nvir), jnp.bfloat16),
            pltpu.VMEM((length, nvir), jnp.bfloat16),
            pltpu.VMEM((nvir, 128), jnp.float32),
            pltpu.SMEM((slots,), jnp.float32),
            pltpu.SMEM((slots,), jnp.float32),
            dma((LOADS,)),
        ]
        + [dma((rounds,))] * 6
        + [dma((3, rounds))] * 2
        + [dma((rounds,))] * 4,
        compiler_params=pltpu.CompilerParams(
            collective_id=0, has_side_effects=True, vmem_limit_bytes=58 * 1024 * 1024
        ),
    )(occ_energy, pair_list, pair_count, block_mask, virt_energy[None, :], virt_coef, half_factors)

    steps = 4
    part = slab // steps
    wide_rows = pl.pallas_call(
        last_kernel,
        out_shape=jax.ShapeDtypeStruct((slab * rounds, nao), jnp.float32),
        grid=(steps,),
        in_specs=[
            pl.BlockSpec((rounds, part, nvir), lambda n: (0, n, 0)),
            pl.BlockSpec((nao, nvir), lambda n: (0, 0)),
        ],
        out_specs=pl.BlockSpec((part * rounds, nao), lambda n: (n, 0)),
        scratch_shapes=[pltpu.VMEM((nao // 128, part * rounds, 128), jnp.float32)],
        compiler_params=pltpu.CompilerParams(vmem_limit_bytes=32 * 1024 * 1024),
    )(back, virt_coef)
    return wide_rows.reshape(slab, rounds, nao)


def solution(mesh):
    in_specs = (P("aux", "obat", None), P("obat", None), P(), P(), P(), P(), P())
    out_specs = P("aux", "obat", None)
    return jax.shard_map(
        on_device, mesh=mesh, in_specs=in_specs, out_specs=out_specs, check_vma=False
    )
```

time: 147 us -> 112 us (0.76)
  Pallas kernels: 120 us -> 109 us
  local copies, waits for them, and re-layouts: 12.9 us -> 3.08 us
  matrix products: 6.74 us -> 0 us
  other arithmetic: 6.06 us -> 0 us
    pallas_call x1, Pallas kernels: 120 us -> 102 us  [on_device(): pl.pallas_call(pair_kernel, out_shape=jax.ShapeDtypeStruct((rounds, slab,...]
    dot_general x2 -> x0, matrix products: 6.74 us -> none  [the longest x1 3.42 us: on_device(): jnp.einsum('ipa,ma->pim', back, virt_coef, preferred_element_type=jnp.flo...]
    pallas_call x0 -> x1, Pallas kernels: none -> 6.44 us  [on_device(): pl.pallas_call(last_kernel, out_shape=jax.ShapeDtypeStruct((slab * rounds...]
    transpose x1 -> x0, local copies, waits for them, and re-layouts: 6.35 us -> none  [on_device(): jnp.einsum('ipa,ma->pim', back, virt_coef, preferred_element_type=jnp.flo...]
    dynamic_slice x3 -> x0, local copies, waits for them, and re-layouts: 3.5 us -> none  [the longest x1 1.32 us: on_device(): used = jnp.arange(pair_list.shape[1]) < pair_count[orbital]]
    unnamed x2 -> x5, local copies, waits for them, and re-layouts: 0.01 us -> 3.08 us
    mul x1 -> x0, other arithmetic: 2.1 us -> none  [on_device(): masked = half_factors * expand[None, :, :]]
    broadcast_in_dim x2 -> x0, local copies, waits for them, and re-layouts: 1.66 us -> none  [the longest x1 1.56 us: on_device(): virt_energy[:, None]]
where the time goes in v3:
time: 112 us
  Pallas kernels  109 us (97%)
  local copies, waits for them, and re-layouts  3.08 us (3%)
    pallas_call x1, Pallas kernels, on_device(): pl.pallas_call(pair_kernel, out_shape=jax.ShapeDtypeStruct((rounds, slab,...  102 us
    pallas_call x1, Pallas kernels, on_device(): pl.pallas_call(last_kernel, out_shape=jax.ShapeDtypeStruct((slab * rounds...  6.44 us
    unnamed x5, local copies, waits for them, and re-layouts  3.08 us

profile of v3, /device:TPU:0, one launch (start us, length us, event | category | flops | bytes accessed | tf_op | source)
XLA Modules:
  0.0 111.6 jit_solution(861607428366469887)
XLA Ops:
  0.0 0.0 copy-start.1
  0.0 1.5 %copy.8.listed = s32[128,6]{1,0:T(8,128)} copy(s32[128,6]{0,1:T(8,128)} %param.12) | data formatting | bytes 6144 | tf_op args[5]
  1.5 102.1 %shard_map.73.back = bf16[16,128,512]{2,1,0:T(8,128)(2,1)} custom-call(f32[128]{0:T(128)} %occ.1, s32[128,6]{1,0:T(8,128)} %copy.8.listed, s32[128]{0:T(128)} %counted.1, s32[16,12]{1,0:T(8,128)} %mask.1, f32[1,512]{1,0:T(1,128)} %bitcast.2, bf16[768,512]{1,0:T(8,128)(2,1)} %virt.3, bf16[128,16,768]{2,1,0:T(8,128)(2,1)} %half.1), custom_call_target="tpu_custom_call" | custom-call | tf_op jit(solution)/shard_map/pallas_call | solution.py:297
  103.6 0.0 copy-done.1
  103.6 0.0 copy-start
  103.6 1.6 %copy-done = bf16[16,128,512]{2,1,0:T(8,128)(2,1)S(1)} copy-done((bf16[16,128,512]{2,1,0:T(8,128)(2,1)S(1)}, bf16[16,128,512]{2,1,0:T(8,128)(2,1)}, u32[]{:S(2)}) %copy-start) | copy-done | bytes 2097176
  105.2 6.4 %shard_map.74 = f32[2048,768]{1,0:T(8,128)} custom-call(bf16[16,128,512]{2,1,0:T(8,128)(2,1)S(1)} %copy-done, bf16[768,512]{1,0:T(8,128)(2,1)S(1)} %copy-done.1), custom_call_target="tpu_custom_call" | custom-call | tf_op jit(solution)/shard_map/pallas_call | solution.py:328
Async XLA Ops:
  0.0 103.6 %copy-start.1 = (bf16[768,512]{1,0:T(8,128)(2,1)S(1)}, bf16[768,512]{1,0:T(8,128)(2,1)}, u32[]{:S(2)}) copy-start(bf16[768,512]{1,0:T(8,128)(2,1)} %virt.3) | copy-start | bytes 2359300
  103.6 1.6 %copy-start = (bf16[16,128,512]{2,1,0:T(8,128)(2,1)S(1)}, bf16[16,128,512]{2,1,0:T(8,128)(2,1)}, u32[]{:S(2)}) copy-start(bf16[16,128,512]{2,1,0:T(8,128)(2,1)} %shard_map.73.back) | copy-start | bytes 6291460

commit v4 on v3

--- a/solution.py
+++ b/solution.py
@@ -8,8 +8,14 @@
 AOBLK = 64
 SIDE = 4
 AHEAD = 3
-LAG_NEAR, LAG_FAR = 1, 2
+LAG_NEAR, LAG_FAR = 2, 3
+LAG_SHARE = 2
 LOADS = 4
+ROWS = 16
+SHIFTS = (
+    (0, 0), (0, 1), (1, 0), (0, 3), (3, 0), (1, 1), (3, 3), (1, 3),
+    (3, 1), (0, 2), (2, 0), (1, 2), (2, 1), (3, 2), (2, 3), (2, 2),
+)
 MESH = pl.DeviceIdType.MESH
 
 
@@ -17,10 +23,20 @@
     return lax.dot_general(a, b, (contract, ((), ())), preferred_element_type=jnp.float32)
 
 
+def look_up(axis, r):
+    if isinstance(r, int):
+        return SHIFTS[r][axis]
+    found = jnp.int32(0)
+    for k, steps in enumerate(SHIFTS):
+        if steps[axis]:
+            found += jnp.where(r == k, steps[axis], 0)
+    return found
+
+
 def pair_kernel(
-    occ, listed, counted, mask, virt_row, virt, half, out,
-    half_vm, wide_f, local, panels, total, recip, mixed, share, opposite, gamma, virt_col, sums, weight,
-    l_sem, a_send, a_recv, m_send, m_recv, p_send, p_recv, s_send, s_recv, g_send, g_recv, r_send, r_recv,
+    occ, listed, counted, mask, virt_row, virt, half, out, turned_out,
+    half_vm, wide_f, local, panels, total, recip, mixed, share, opposite, gamma, virt_col, turned, sums, weight,
+    l_sem, t_sem, a_send, a_recv, m_send, m_recv, p_send, p_recv, s_send, s_recv, g_send, g_recv, r_send, r_recv,
 ):
     aux = lax.axis_index("aux")
     obat = lax.axis_index("obat")
@@ -38,7 +54,7 @@
     sibling = (aux, z * 2 + 1 - core)
 
     def shift(r):
-        return (r + r // SIDE) % SIDE, r % SIDE
+        return look_up(0, r), look_up(1, r)
 
     def target(r):
         dy, dx = shift(r)
@@ -50,6 +66,9 @@
 
     def rows(r):
         return pl.ds(pl.multiple_of(r * slab, slab), slab)
+
+    def chunk_rows(c):
+        return pl.ds(pl.multiple_of(c * wide, wide), wide)
 
     def push(src, dst, send, recv, device):
         return pltpu.make_async_remote_copy(
@@ -135,8 +154,8 @@
         for s, (i, j) in enumerate(couples):
             sums[s] = occ[i] + occ[j]
             hit = jnp.int32(0)
-            for p in range(listed.shape[1]):
-                hit += jnp.where((listed[i, p] == j) & (p < counted[i]), 1, 0)
+            for p in range(listed.shape[0]):
+                hit += jnp.where((listed[p, i] == j) & (p < counted[i]), 1, 0)
             weight[s] = hit.astype(jnp.float32)
 
     def prepare(s, carry):
@@ -148,12 +167,14 @@
         return carry
 
     def pair_up(c, held, fixed, others):
-        part = pl.ds(pl.multiple_of(c * wide, wide), wide)
+        part = chunk_rows(c)
         own = panels[fixed, part, :]
         flipped = (-own).T
         for t, s in zip(held, others):
             other = panels[s, part, :]
             total[t] += dot((2 * other).T, own) + dot(flipped, other)
+
+    turned_copy = pltpu.make_async_copy(turned, turned_out, t_sem)
 
     def stage(c, carry):
         @pl.when(c < chunks)
@@ -187,6 +208,8 @@
         @pl.when(c == 0)
         def _():
             virt_col[...] = jnp.broadcast_to(virt_row[...], (128, nvir)).T
+            turned[...] = virt[...].T
+            turned_copy.start()
             prepare_scalars()
             lax.fori_loop(0, slots, prepare, 0)
 
@@ -211,47 +234,48 @@
 
     lax.fori_loop(0, chunks + LAG_FAR, stage, 0)
 
-    def finish(t, carry):
-        s = slots - 1 - t
+    def finish(s, carry):
         mixed[s] = (total[s] * recip[s]).astype(jnp.bfloat16)
         return carry
 
-    lax.fori_loop(0, slots, finish, 0)
-
     halves = [pl.ds(n * (nvir // 2), nvir // 2) for n in range(2)]
 
-    def hand_over(q, carry):
-        length = SIDE * slab
-        quarter = rounds // SIDE - 1 - q
-        part = pl.ds(pl.multiple_of(quarter * length, length), length)
-        for cols in halves:
-            acc = dot(panels[4, part, :], mixed[6, :, cols]) + dot(panels[5, part, :], mixed[7, :, cols])
-            share[part, cols] = acc.astype(jnp.bfloat16)
-        for h in range(SIDE):
-            give(quarter * SIDE + SIDE - 1 - h).start()
-        return carry
-
-    lax.fori_loop(0, rounds // SIDE, hand_over, 0)
-
     def collect(q, carry):
-        c = chunks - 1 - q
-        part = pl.ds(pl.multiple_of(c * wide, wide), wide)
-        give(2 * c + 1).wait_recv()
-        give(2 * c).wait_recv()
-        for cols in halves:
-            acc = opposite[part, cols].astype(jnp.float32)
-            for s in range(6):
-                acc += dot(panels[s, part, :], mixed[s, :, cols])
-            gamma[part, cols] = acc.astype(jnp.bfloat16)
-        back(2 * c + 1).start()
-
-        @pl.when(c > 0)
-        def _():
-            back(2 * c).start()
-
-        return carry
-
-    lax.fori_loop(0, chunks, collect, 0)
+        @pl.when(q < chunks)
+        def _():
+            c = chunks - 1 - q
+            part = chunk_rows(c)
+            for cols in halves:
+                acc = dot(panels[4, part, :], mixed[6, :, cols]) + dot(panels[5, part, :], mixed[7, :, cols])
+                share[part, cols] = acc.astype(jnp.bfloat16)
+            give(2 * c + 1).start()
+            give(2 * c).start()
+
+        @pl.when(q == 0)
+        def _():
+            lax.fori_loop(0, 6, finish, 0)
+
+        @pl.when(q >= LAG_SHARE)
+        def _():
+            c = chunks - 1 - (q - LAG_SHARE)
+            part = chunk_rows(c)
+            give(2 * c + 1).wait_recv()
+            give(2 * c).wait_recv()
+            for cols in halves:
+                acc = opposite[part, cols].astype(jnp.float32)
+                for s in range(6):
+                    acc += dot(panels[s, part, :], mixed[s, :, cols])
+                gamma[part, cols] = acc.astype(jnp.bfloat16)
+            back(2 * c + 1).start()
+
+            @pl.when(c > 0)
+            def _():
+                back(2 * c).start()
+
+        return carry
+
+    lax.fori_loop(6, slots, finish, 0)
+    lax.fori_loop(0, chunks + LAG_SHARE, collect, 0)
     own_copy = pltpu.make_async_copy(gamma.at[pl.ds(0, slab)], out.at[aux], r_send.at[0])
     own_copy.start()
 
@@ -271,18 +295,41 @@
         return carry
 
     own_copy.wait()
+    turned_copy.wait()
     lax.fori_loop(1, rounds, close, 0)
 
 
-def last_kernel(back, virt, out, mixed_rows):
-    batch_rows, part, nvir = back.shape
-    nao = virt.shape[0]
-    product = dot(back[...].reshape(batch_rows * part, nvir), virt[...], ((1,), (1,)))
-    for w in range(nao // 128):
-        cols = slice(w * 128, (w + 1) * 128)
-        for i in range(batch_rows):
-            mixed_rows[w, pl.ds(i, part, stride=batch_rows), :] = product[i * part : (i + 1) * part, cols]
-        out[:, cols] = mixed_rows[w]
+def last_kernel(back, turned, out, back_vm, turned_vm, rows_vm, b_sem, t_sem, o_sem):
+    batch_rows, slab, nvir = back.shape
+    size = batch_rows * ROWS
+    parts = slab // ROWS
+
+    def bring(n):
+        part = pl.ds(n * ROWS, ROWS)
+        return pltpu.make_async_copy(back.at[:, part], back_vm.at[:, part], b_sem.at[n])
+
+    def store(n):
+        part = pl.ds(n * size, size)
+        return pltpu.make_async_copy(rows_vm.at[part], out.at[part], o_sem.at[n])
+
+    turned_copy = pltpu.make_async_copy(turned, turned_vm, t_sem)
+    bring(0).start()
+    turned_copy.start()
+    for n in range(1, parts):
+        bring(n).start()
+    to_row = lax.broadcasted_iota(jnp.int32, (size, size), 0)
+    from_row = lax.broadcasted_iota(jnp.int32, (size, size), 1)
+    order = from_row == to_row % batch_rows * ROWS + to_row // batch_rows
+    order = order.astype(jnp.float32).astype(jnp.bfloat16)
+    turned_copy.wait()
+    for n in range(parts):
+        bring(n).wait()
+        block = back_vm[:, n * ROWS : (n + 1) * ROWS, :].reshape(size, nvir)
+        block = dot(order, block).astype(jnp.bfloat16)
+        rows_vm[n * size : (n + 1) * size, :] = dot(block, turned_vm[...])
+        store(n).start()
+    for n in range(parts):
+        store(n).wait()
 
 
 def on_device(half_factors, block_mask, virt_coef, occ_energy, virt_energy, pair_list, pair_count):
@@ -294,11 +341,14 @@
     smem = pl.BlockSpec(memory_space=pltpu.SMEM)
     vmem = pl.BlockSpec(memory_space=pltpu.VMEM)
     anywhere = pl.BlockSpec(memory_space=pl.ANY)
-    back = pl.pallas_call(
+    back, turned = pl.pallas_call(
         pair_kernel,
-        out_shape=jax.ShapeDtypeStruct((rounds, slab, nvir), jnp.bfloat16),
+        out_shape=(
+            jax.ShapeDtypeStruct((rounds, slab, nvir), jnp.bfloat16),
+            jax.ShapeDtypeStruct((nvir, nao), jnp.bfloat16),
+        ),
         in_specs=[smem, smem, smem, vmem, vmem, vmem, anywhere],
-        out_specs=anywhere,
+        out_specs=(anywhere, anywhere),
         scratch_shapes=[
             pltpu.VMEM((slab, rounds, nao), jnp.bfloat16),
             pltpu.VMEM((nvir // 128, length, 128), jnp.float32),
@@ -311,9 +361,11 @@
             pltpu.VMEM((length, nvir), jnp.bfloat16),
             pltpu.VMEM((length, nvir), jnp.bfloat16),
             pltpu.VMEM((nvir, 128), jnp.float32),
+            pltpu.VMEM((nvir, nao), jnp.bfloat16),
             pltpu.SMEM((slots,), jnp.float32),
             pltpu.SMEM((slots,), jnp.float32),
             dma((LOADS,)),
+            dma,
         ]
         + [dma((rounds,))] * 6
         + [dma((3, rounds))] * 2
@@ -321,22 +373,24 @@
         compiler_params=pltpu.CompilerParams(
             collective_id=0, has_side_effects=True, vmem_limit_bytes=58 * 1024 * 1024
         ),
-    )(occ_energy, pair_list, pair_count, block_mask, virt_energy[None, :], virt_coef, half_factors)
-
-    steps = 4
-    part = slab // steps
+    )(occ_energy, pair_list.T, pair_count, block_mask, virt_energy[None, :], virt_coef, half_factors)
+
+    parts = slab // ROWS
     wide_rows = pl.pallas_call(
         last_kernel,
-        out_shape=jax.ShapeDtypeStruct((slab * rounds, nao), jnp.float32),
-        grid=(steps,),
-        in_specs=[
-            pl.BlockSpec((rounds, part, nvir), lambda n: (0, n, 0)),
-            pl.BlockSpec((nao, nvir), lambda n: (0, 0)),
+        out_shape=jax.ShapeDtypeStruct((length, nao), jnp.float32),
+        in_specs=[anywhere, anywhere],
+        out_specs=anywhere,
+        scratch_shapes=[
+            pltpu.VMEM((rounds, slab, nvir), jnp.bfloat16),
+            pltpu.VMEM((nvir, nao), jnp.bfloat16),
+            pltpu.VMEM((length, nao), jnp.float32),
+            dma((parts,)),
+            dma,
+            dma((parts,)),
         ],
-        out_specs=pl.BlockSpec((part * rounds, nao), lambda n: (n, 0)),
-        scratch_shapes=[pltpu.VMEM((nao // 128, part * rounds, 128), jnp.float32)],
-        compiler_params=pltpu.CompilerParams(vmem_limit_bytes=32 * 1024 * 1024),
-    )(back, virt_coef)
+        compiler_params=pltpu.CompilerParams(vmem_limit_bytes=60 * 1024 * 1024),
+    )(back, turned)
     return wide_rows.reshape(slab, rounds, nao)
 
 

time: 112 us -> 104 us (0.929)
  Pallas kernels: 109 us -> 103 us
  local copies, waits for them, and re-layouts: 3.08 us -> 0 us
    pallas_call x2, Pallas kernels: 109 us -> 103 us  [the longest x1 95.7 us: on_device(): pl.pallas_call(pair_kernel, out_shape=(jax.ShapeDtypeStruct((rounds, slab...]
    unnamed x5 -> x0, local copies, waits for them, and re-layouts: 3.08 us -> none
where the time goes in v4:
time: 104 us; the launch traced here: 103 us
  Pallas kernels  103 us (99%)
    pallas_call x1, Pallas kernels, on_device(): pl.pallas_call(pair_kernel, out_shape=(jax.ShapeDtypeStruct((rounds, slab...  95.7 us
    pallas_call x1, Pallas kernels, on_device(): pl.pallas_call(last_kernel, out_shape=jax.ShapeDtypeStruct((length, nao),...  7.06 us

profile of v4, /device:TPU:0, one launch (start us, length us, event | category | flops | bytes accessed | tf_op | source)
XLA Modules:
  0.0 102.8 jit_solution(11233447512343217131)
XLA Ops:
  0.0 95.7 %shard_map.73 = (bf16[16,128,512]{2,1,0:T(8,128)(2,1)}, bf16[512,768]{1,0:T(8,128)(2,1)}) custom-call(f32[128]{0:T(128)} %occ.1, s32[6,128]{1,0:T(8,128)} %bitcast.3, s32[128]{0:T(128)} %counted.1, s32[16,12]{1,0:T(8,128)} %mask.1, f32[1,512]{1,0:T(1,128)} %bitcast.4, bf16[768,512]{1,0:T(8,128)(2,1)} %virt.1, bf16[128,16,768]{2,1,0:T(8,128)(2,1)} %half.1), custom_call_target="tpu_custom_call" | custom-call | tf_op jit(solution)/shard_map/pallas_call | solution.py:344
  95.7 7.1 %shard_map.74 = f32[2048,768]{1,0:T(8,128)} custom-call(bf16[16,128,512]{2,1,0:T(8,128)(2,1)} %get-tuple-element.7.back, bf16[512,768]{1,0:T(8,128)(2,1)} %get-tuple-element.8.turned), custom_call_target="tpu_custom_call" | custom-call | tf_op jit(solution)/shard_map/pallas_call | solution.py:379

commit v5 on v4

--- a/solution.py
+++ b/solution.py
@@ -9,7 +9,8 @@
 SIDE = 4
 AHEAD = 3
 LAG_NEAR, LAG_FAR = 2, 3
-LAG_SHARE = 2
+SPAN = 1
+LAG_SHARE = 3
 LOADS = 4
 ROWS = 16
 SHIFTS = (
@@ -34,9 +35,9 @@
 
 
 def pair_kernel(
-    occ, listed, counted, mask, virt_row, virt, half, out, turned_out,
-    half_vm, wide_f, local, panels, total, recip, mixed, share, opposite, gamma, virt_col, turned, sums, weight,
-    l_sem, t_sem, a_send, a_recv, m_send, m_recv, p_send, p_recv, s_send, s_recv, g_send, g_recv, r_send, r_recv,
+    occ, listed, counted, mask, virt_row, virt, half, out,
+    half_vm, wide_f, local, panels, total, recip, mixed, share, opposite, gamma, virt_col, order, arrived, lined_up, sums, weight,
+    l_sem, o_sem, a_send, a_recv, m_send, m_recv, p_send, p_recv, s_send, s_recv, g_send, g_recv, r_send, r_recv,
 ):
     aux = lax.axis_index("aux")
     obat = lax.axis_index("obat")
@@ -95,7 +96,7 @@
         return push(share.at[rows(r)], opposite.at[rows(r)], g_send.at[r], g_recv.at[r], one)
 
     def back(r):
-        return push(gamma.at[rows(r)], out.at[aux], r_send.at[r], r_recv.at[r], (source(r), obat))
+        return push(gamma.at[rows(r)], arrived.at[aux], r_send.at[r], r_recv.at[r], (source(r), obat))
 
     piece = slab // LOADS
 
@@ -174,7 +175,13 @@
             other = panels[s, part, :]
             total[t] += dot((2 * other).T, own) + dot(flipped, other)
 
-    turned_copy = pltpu.make_async_copy(turned, turned_out, t_sem)
+    size = rounds * ROWS
+
+    def plan_order():
+        to_row = lax.broadcasted_iota(jnp.int32, (size, size), 0)
+        from_row = lax.broadcasted_iota(jnp.int32, (size, size), 1)
+        hit = from_row == to_row % rounds * ROWS + to_row // rounds
+        order[...] = hit.astype(jnp.float32).astype(jnp.bfloat16)
 
     def stage(c, carry):
         @pl.when(c < chunks)
@@ -208,8 +215,7 @@
         @pl.when(c == 0)
         def _():
             virt_col[...] = jnp.broadcast_to(virt_row[...], (128, nvir)).T
-            turned[...] = virt[...].T
-            turned_copy.start()
+            plan_order()
             prepare_scalars()
             lax.fori_loop(0, slots, prepare, 0)
 
@@ -240,16 +246,21 @@
 
     halves = [pl.ds(n * (nvir // 2), nvir // 2) for n in range(2)]
 
+    steps = rounds // SPAN
+
+    def span_rows(c):
+        return pl.ds(pl.multiple_of(c * SPAN * slab, SPAN * slab), SPAN * slab)
+
     def collect(q, carry):
-        @pl.when(q < chunks)
-        def _():
-            c = chunks - 1 - q
-            part = chunk_rows(c)
+        @pl.when(q < steps)
+        def _():
+            c = steps - 1 - q
+            part = span_rows(c)
             for cols in halves:
                 acc = dot(panels[4, part, :], mixed[6, :, cols]) + dot(panels[5, part, :], mixed[7, :, cols])
                 share[part, cols] = acc.astype(jnp.bfloat16)
-            give(2 * c + 1).start()
-            give(2 * c).start()
+            for h in range(SPAN):
+                give(SPAN * c + SPAN - 1 - h).start()
 
         @pl.when(q == 0)
         def _():
@@ -257,27 +268,42 @@
 
         @pl.when(q >= LAG_SHARE)
         def _():
-            c = chunks - 1 - (q - LAG_SHARE)
-            part = chunk_rows(c)
-            give(2 * c + 1).wait_recv()
-            give(2 * c).wait_recv()
+            c = steps - 1 - (q - LAG_SHARE)
+            part = span_rows(c)
+            for h in range(SPAN):
+                give(SPAN * c + SPAN - 1 - h).wait_recv()
             for cols in halves:
                 acc = opposite[part, cols].astype(jnp.float32)
                 for s in range(6):
                     acc += dot(panels[s, part, :], mixed[s, :, cols])
                 gamma[part, cols] = acc.astype(jnp.bfloat16)
-            back(2 * c + 1).start()
-
-            @pl.when(c > 0)
-            def _():
-                back(2 * c).start()
+            for h in range(SPAN):
+                r = SPAN * c + SPAN - 1 - h
+
+                @pl.when(r > 0)
+                def _():
+                    back(r).start()
 
         return carry
 
     lax.fori_loop(6, slots, finish, 0)
-    lax.fori_loop(0, chunks + LAG_SHARE, collect, 0)
-    own_copy = pltpu.make_async_copy(gamma.at[pl.ds(0, slab)], out.at[aux], r_send.at[0])
-    own_copy.start()
+    lax.fori_loop(0, steps + LAG_SHARE, collect, 0)
+    arrived[aux] = gamma[pl.ds(0, slab), :]
+
+    def land(r, carry):
+        back(rounds - r).wait_recv()
+        return carry
+
+    lax.fori_loop(1, rounds, land, 0)
+
+    def leave(n):
+        part = pl.ds(n * size, size)
+        return pltpu.make_async_copy(lined_up.at[part], out.at[part], o_sem.at[n])
+
+    for n in range(slab // ROWS):
+        block = arrived[:, n * ROWS : (n + 1) * ROWS, :].reshape(size, nvir)
+        lined_up[pl.ds(n * size, size), :] = dot(order[...], block).astype(jnp.bfloat16)
+        leave(n).start()
 
     def settle(r, carry):
         to_one(r).wait_send()
@@ -291,45 +317,12 @@
 
     def close(r, carry):
         scatter(r).wait_send()
-        back(r).wait()
-        return carry
-
-    own_copy.wait()
-    turned_copy.wait()
+        back(r).wait_send()
+        return carry
+
     lax.fori_loop(1, rounds, close, 0)
-
-
-def last_kernel(back, turned, out, back_vm, turned_vm, rows_vm, b_sem, t_sem, o_sem):
-    batch_rows, slab, nvir = back.shape
-    size = batch_rows * ROWS
-    parts = slab // ROWS
-
-    def bring(n):
-        part = pl.ds(n * ROWS, ROWS)
-        return pltpu.make_async_copy(back.at[:, part], back_vm.at[:, part], b_sem.at[n])
-
-    def store(n):
-        part = pl.ds(n * size, size)
-        return pltpu.make_async_copy(rows_vm.at[part], out.at[part], o_sem.at[n])
-
-    turned_copy = pltpu.make_async_copy(turned, turned_vm, t_sem)
-    bring(0).start()
-    turned_copy.start()
-    for n in range(1, parts):
-        bring(n).start()
-    to_row = lax.broadcasted_iota(jnp.int32, (size, size), 0)
-    from_row = lax.broadcasted_iota(jnp.int32, (size, size), 1)
-    order = from_row == to_row % batch_rows * ROWS + to_row // batch_rows
-    order = order.astype(jnp.float32).astype(jnp.bfloat16)
-    turned_copy.wait()
-    for n in range(parts):
-        bring(n).wait()
-        block = back_vm[:, n * ROWS : (n + 1) * ROWS, :].reshape(size, nvir)
-        block = dot(order, block).astype(jnp.bfloat16)
-        rows_vm[n * size : (n + 1) * size, :] = dot(block, turned_vm[...])
-        store(n).start()
-    for n in range(parts):
-        store(n).wait()
+    for n in range(slab // ROWS):
+        leave(n).wait()
 
 
 def on_device(half_factors, block_mask, virt_coef, occ_energy, virt_energy, pair_list, pair_count):
@@ -341,14 +334,11 @@
     smem = pl.BlockSpec(memory_space=pltpu.SMEM)
     vmem = pl.BlockSpec(memory_space=pltpu.VMEM)
     anywhere = pl.BlockSpec(memory_space=pl.ANY)
-    back, turned = pl.pallas_call(
+    back = pl.pallas_call(
         pair_kernel,
-        out_shape=(
-            jax.ShapeDtypeStruct((rounds, slab, nvir), jnp.bfloat16),
-            jax.ShapeDtypeStruct((nvir, nao), jnp.bfloat16),
-        ),
+        out_shape=jax.ShapeDtypeStruct((length, nvir), jnp.bfloat16),
         in_specs=[smem, smem, smem, vmem, vmem, vmem, anywhere],
-        out_specs=(anywhere, anywhere),
+        out_specs=anywhere,
         scratch_shapes=[
             pltpu.VMEM((slab, rounds, nao), jnp.bfloat16),
             pltpu.VMEM((nvir // 128, length, 128), jnp.float32),
@@ -361,11 +351,13 @@
             pltpu.VMEM((length, nvir), jnp.bfloat16),
             pltpu.VMEM((length, nvir), jnp.bfloat16),
             pltpu.VMEM((nvir, 128), jnp.float32),
-            pltpu.VMEM((nvir, nao), jnp.bfloat16),
+            pltpu.VMEM((rounds * ROWS, rounds * ROWS), jnp.bfloat16),
+            pltpu.VMEM((rounds, slab, nvir), jnp.bfloat16),
+            pltpu.VMEM((length, nvir), jnp.bfloat16),
             pltpu.SMEM((slots,), jnp.float32),
             pltpu.SMEM((slots,), jnp.float32),
             dma((LOADS,)),
-            dma,
+            dma((slab // ROWS,)),
         ]
         + [dma((rounds,))] * 6
         + [dma((3, rounds))] * 2
@@ -375,22 +367,7 @@
         ),
     )(occ_energy, pair_list.T, pair_count, block_mask, virt_energy[None, :], virt_coef, half_factors)
 
-    parts = slab // ROWS
-    wide_rows = pl.pallas_call(
-        last_kernel,
-        out_shape=jax.ShapeDtypeStruct((length, nao), jnp.float32),
-        in_specs=[anywhere, anywhere],
-        out_specs=anywhere,
-        scratch_shapes=[
-            pltpu.VMEM((rounds, slab, nvir), jnp.bfloat16),
-            pltpu.VMEM((nvir, nao), jnp.bfloat16),
-            pltpu.VMEM((length, nao), jnp.float32),
-            dma((parts,)),
-            dma,
-            dma((parts,)),
-        ],
-        compiler_params=pltpu.CompilerParams(vmem_limit_bytes=60 * 1024 * 1024),
-    )(back, turned)
+    wide_rows = dot(back, virt_coef, ((1,), (1,)))
     return wide_rows.reshape(slab, rounds, nao)
 
 

time: 104 us -> 103 us (level)
  Pallas kernels: 103 us -> 95.4 us
  matrix products: 0 us -> 6.13 us
    pallas_call x2 -> x1, Pallas kernels: 103 us -> 95.4 us  [on_device(): pl.pallas_call(pair_kernel, out_shape=jax.ShapeDtypeStruct((length, nvir)...]
    dot_general x0 -> x1, matrix products: none -> 6.13 us  [dot(): lax.dot_general(a, b, (contract, ((), ())), preferred_element_type=jnp.fl...]
where the time goes in v5:
time: 103 us; the launch traced here: 102 us
  Pallas kernels  95.4 us (93%)
  matrix products  6.13 us (6%)
    pallas_call x1, Pallas kernels, on_device(): pl.pallas_call(pair_kernel, out_shape=jax.ShapeDtypeStruct((length, nvir)...  95.4 us
    dot_general x1, matrix products, dot(): lax.dot_general(a, b, (contract, ((), ())), preferred_element_type=jnp.fl...  6.13 us

profile of v5, /device:TPU:0, one launch (start us, length us, event | category | flops | bytes accessed | tf_op | source)
XLA Modules:
  0.0 101.5 jit_solution(14871423769297341945)
XLA Ops:
  0.0 0.0 copy-start
  0.0 95.4 %shard_map.73 = bf16[2048,512]{1,0:T(8,128)(2,1)} custom-call(f32[128]{0:T(128)} %occ.1, s32[6,128]{1,0:T(8,128)} %bitcast.5, s32[128]{0:T(128)} %counted.1, s32[16,12]{1,0:T(8,128)} %mask.1, f32[1,512]{1,0:T(1,128)} %bitcast.6, bf16[768,512]{1,0:T(8,128)(2,1)} %virt.1, bf16[128,16,768]{2,1,0:T(8,128)(2,1)} %half.1), custom_call_target="tpu_custom_call" | custom-call | tf_op jit(solution)/shard_map/pallas_call | solution.py:337
  95.4 0.0 copy-done
  95.4 6.1 %fusion = f32[2048,768]{1,0:T(8,128)} fusion(bf16[2048,512]{1,0:T(8,128)(2,1)} %shard_map.73, bf16[768,512]{1,0:T(8,128)(2,1)S(1)} %copy-done), kind=kOutput, calls=%fused_computation | convolution fusion | flops 1610612736 | bytes 9175040 | tf_op jit(solution)/shard_map/dot_general | solution.py:24
Async XLA Ops:
  0.0 95.4 %copy-start = (bf16[768,512]{1,0:T(8,128)(2,1)S(1)}, bf16[768,512]{1,0:T(8,128)(2,1)}, u32[]{:S(2)}) copy-start(bf16[768,512]{1,0:T(8,128)(2,1)} %virt.1) | copy-start | bytes 2359300

commit v6 on v5

--- a/solution.py
+++ b/solution.py
@@ -8,7 +8,7 @@
 AOBLK = 64
 SIDE = 4
 AHEAD = 3
-LAG_NEAR, LAG_FAR = 2, 3
+LAG_OWN, LAG_NEAR, LAG_FAR = 1, 2, 3
 SPAN = 1
 LAG_SHARE = 3
 LOADS = 4
@@ -203,38 +203,40 @@
             for h in range(2):
                 send_out(2 * (c + AHEAD) + h, 0)
 
+        @pl.when(c == 0)
+        def _():
+            virt_col[...] = jnp.broadcast_to(virt_row[...], (128, nvir)).T
+            plan_order()
+            prepare_scalars()
+            lax.fori_loop(0, slots, prepare, 0)
+
+        @pl.when((c >= LAG_OWN) & (c < chunks + LAG_OWN))
+        def _():
+            b = c - LAG_OWN
+            for h in range(2):
+                across(0, 2 * b + h).wait_recv()
+            pair_up(b, (0, 1), 0, (0, 1))
+
+        @pl.when(c >= LAG_FAR)
+        def _():
+            b = c - LAG_FAR
+            for h in range(2):
+                across(1, 2 * b + h).wait_recv()
+                across(2, 2 * b + h).wait_recv()
+            pair_up(b, (3, 5), 0, (3, 5))
+            pair_up(b, (7,), 2, (5,))
+
         @pl.when((c >= LAG_NEAR) & (c < chunks + LAG_NEAR))
         def _():
-            for h in range(2):
-                r = 2 * (c - LAG_NEAR) + h
+            b = c - LAG_NEAR
+            for h in range(2):
+                r = 2 * b + h
                 to_two(r).wait_recv()
                 across(1, r).start()
                 to_one(r).wait_recv()
                 across(2, r).start()
-
-        @pl.when(c == 0)
-        def _():
-            virt_col[...] = jnp.broadcast_to(virt_row[...], (128, nvir)).T
-            plan_order()
-            prepare_scalars()
-            lax.fori_loop(0, slots, prepare, 0)
-
-        @pl.when((c >= LAG_NEAR) & (c < chunks + LAG_NEAR))
-        def _():
-            b = c - LAG_NEAR
-            for h in range(2):
-                across(0, 2 * b + h).wait_recv()
-            pair_up(b, (0, 1, 2, 4), 0, (0, 1, 2, 4))
+            pair_up(b, (2, 4), 0, (2, 4))
             pair_up(b, (6,), 2, (4,))
-
-        @pl.when(c >= LAG_FAR)
-        def _():
-            b = c - LAG_FAR
-            for h in range(2):
-                across(1, 2 * b + h).wait_recv()
-                across(2, 2 * b + h).wait_recv()
-            pair_up(b, (3, 5), 0, (3, 5))
-            pair_up(b, (7,), 2, (5,))
 
         return carry
 

time: 103 us -> 110 us (1.068)
  the two profiles are of different devices: /device:TPU:0 before, /device:TPU:37 now
where the time goes in v6:
time: 110 us
  Pallas kernels  103 us (94%)
  matrix products  6.12 us (6%)
    pallas_call x1, Pallas kernels, on_device(): pl.pallas_call(pair_kernel, out_shape=jax.ShapeDtypeStruct((length, nvir)...  103 us
    dot_general x1, matrix products, dot(): lax.dot_general(a, b, (contract, ((), ())), preferred_element_type=jnp.fl...  6.12 us

profile of v6, /device:TPU:37, one launch (start us, length us, event | category | flops | bytes accessed | tf_op | source)
XLA Modules:
  0.0 109.6 jit_solution(16208870073453856809)
XLA Ops:
  0.0 0.0 copy-start
  0.0 103.4 %shard_map.73 = bf16[2048,512]{1,0:T(8,128)(2,1)} custom-call(f32[128]{0:T(128)} %occ.1, s32[6,128]{1,0:T(8,128)} %bitcast.5, s32[128]{0:T(128)} %counted.1, s32[16,12]{1,0:T(8,128)} %mask.1, f32[1,512]{1,0:T(1,128)} %bitcast.6, bf16[768,512]{1,0:T(8,128)(2,1)} %virt.1, bf16[128,16,768]{2,1,0:T(8,128)(2,1)} %half.1), custom_call_target="tpu_custom_call" | custom-call | tf_op jit(solution)/shard_map/pallas_call | solution.py:339
  103.4 0.0 copy-done
  103.4 6.1 %fusion = f32[2048,768]{1,0:T(8,128)} fusion(bf16[2048,512]{1,0:T(8,128)(2,1)} %shard_map.73, bf16[768,512]{1,0:T(8,128)(2,1)S(1)} %copy-done), kind=kOutput, calls=%fused_computation | convolution fusion | flops 1610612736 | bytes 9175040 | tf_op jit(solution)/shard_map/dot_general | solution.py:24
Async XLA Ops:
  0.0 103.4 %copy-start = (bf16[768,512]{1,0:T(8,128)(2,1)S(1)}, bf16[768,512]{1,0:T(8,128)(2,1)}, u32[]{:S(2)}) copy-start(bf16[768,512]{1,0:T(8,128)(2,1)} %virt.1) | copy-start | bytes 2359300
